TPU v7x, 32 devices: a whole 2x2x4 slice. The times are simulated.
32 devices in a mesh: ctx: 8 (over y, x, core), tp: 4 (over z).
Axes of the slice: x: 2, y: 2, z: 4, core: 2. Of those that a mesh axis runs over, the one named last changes fastest.
Arguments:
- residual: bfloat16 [2048, 4096], P('ctx', 'tp'), may hold values from -6 to 6
- proj: bfloat16 [2048, 3, 4096], P('ctx', None, 'tp'), may hold values from -5 to 5
- short_filter: bfloat16 [7, 3, 4096], P(None, None, 'tp'), may hold values from -2.5 to 2.5
- medium_filter: bfloat16 [128, 4096], P(None, 'tp'), may hold values from -4 to 4
- skip: float32 [4096], P('tp'), may hold values from -3 to 3
- out_weight: bfloat16 [4096, 4096], P('ctx', 'tp'), may hold values from -0.09375 to 0.09375
Outputs:
- block_out: bfloat16 [2048, 4096], P('ctx', 'tp')
All inputs are finite; a program needn't handle non-finite values.
Results may differ from a plain program's by a relative error of at most 0.0085.
Values may be sent and summed in bfloat16 or wider, within the bound.
A program may use at most 64 MiB of HBM per device.

v0:
```python
import jax
import jax.numpy as jnp
from jax import lax
from jax.sharding import PartitionSpec as P

BLOCK = 32


def passed_along(array, axis, by):
    devices = lax.axis_size(axis)
    pairs = [(i, i + by) for i in range(devices) if 0 <= i + by < devices]
    return lax.ppermute(array, axis, pairs)


def short_mix(extended, short_filter, count):
    taps = short_filter.shape[0]
    wide = extended.astype(jnp.float32)
    mixed = jnp.zeros((count,) + extended.shape[1:], jnp.float32)
    for j in range(taps):
        mixed = (
            mixed + short_filter[j].astype(jnp.float32) * wide[taps - 1 - j : taps - 1 - j + count]
        )
    return mixed


def medium_mix(extended, medium_filter, count):
    reach = medium_filter.shape[0]
    chans = extended.shape[1]
    blocks = extended.reshape((count + reach) // BLOCK, BLOCK, chans)
    nblocks = count // BLOCK
    windows = jnp.concatenate([blocks[i : i + nblocks] for i in range(reach // BLOCK + 1)], axis=1)
    out_pos = lax.broadcasted_iota(jnp.int32, (BLOCK, BLOCK + reach, reach), 0)
    win_pos = lax.broadcasted_iota(jnp.int32, (BLOCK, BLOCK + reach, reach), 1)
    tap_pos = lax.broadcasted_iota(jnp.int32, (BLOCK, BLOCK + reach, reach), 2)
    select = (out_pos + reach - win_pos == tap_pos).astype(jnp.bfloat16)
    banded = jnp.einsum(
        "bwj,jc->bwc", select, medium_filter, preferred_element_type=jnp.float32
    ).astype(jnp.bfloat16)
    filtered = jnp.einsum("bwc,awc->abc", banded, windows, preferred_element_type=jnp.float32)
    return filtered.reshape(count, chans)


def on_device(residual, proj, short_filter, medium_filter, skip, out_weight):
    rows = proj.shape[0]
    chans = proj.shape[2]
    taps = short_filter.shape[0]
    reach = medium_filter.shape[0]
    depth = reach + taps - 2
    before = passed_along(proj[rows - depth :], "ctx", 1)
    mixed = short_mix(jnp.concatenate([before, proj], 0), short_filter, rows + reach - 1)
    product = (mixed[:, 1] * mixed[:, 2]).astype(jnp.bfloat16)
    extended = jnp.concatenate([jnp.zeros((1, chans), jnp.bfloat16), product], 0)
    query = mixed[reach - 1 :, 0]
    current = product[reach - 1 :]
    filtered = medium_mix(extended, medium_filter, rows)
    filtered = filtered + skip * current.astype(jnp.float32)
    gated = (query * filtered).astype(jnp.bfloat16)
    whole = lax.all_gather(gated, "tp", axis=1, tiled=True)
    total = jnp.dot(
        whole,
        lax.all_gather(out_weight, "ctx", axis=0, tiled=True),
        preferred_element_type=jnp.float32,
    )
    return (residual.astype(jnp.float32) + total).astype(jnp.bfloat16)


def solution(mesh):
    in_specs = (
        P("ctx", "tp"),
        P("ctx", None, "tp"),
        P(None, None, "tp"),
        P(None, "tp"),
        P("tp"),
        P("ctx", "tp"),
    )
    out_specs = P("ctx", "tp")
    return jax.shard_map(
        on_device, mesh=mesh, in_specs=in_specs, out_specs=out_specs, check_vma=False
    )
```

profile of v0, /device:TPU:1, one launch (start us, length us, event | category | flops | bytes accessed | tf_op | source)
XLA Modules:
  0.0 211.9 jit_solution(12874010557583197253)
XLA Ops:
  6.5 0.0 copy-start
  6.5 0.0 all-gather.3.cloned.1.call-start
  6.5 1.4 slice.94
  8.0 4.5 %collective-permute-start = (bf16[133,3,1024]{2,0,1:T(8,128)(2,1)S(1)}, bf16[133,3,1024]{2,0,1:T(8,128)(2,1)S(1)}, u32[]{:S(2)}, u32[]{:S(2)}) collective-permute-start(bf16[133,3,1024]{2,0,1:T(8,128)(2,1)S(1)} %slice.94), channel_id=1, source_target_pairs={{0,4},{4,8},{8,12},{12,16},{16,20},{20,24},{24,28},{1,5},{5,9},{9,... | collective-permute-start | bytes 2451464 | tf_op jit(solution)/shard_map/ppermute | solution.py:12
  12.5 0.0 copy-done
  12.5 0.0 copy-start.4
  12.5 5.5 %fusion.8 = bf16[32,160,1024]{2,1,0:T(8,128)(2,1)} fusion(s32[32]{0:T(128)S(1)} %iota_add_fusion, bf16[128,1024]{1,0:T(8,128)(2,1)S(1)} %copy-done), kind=kOutput, calls=%fused_computation.16 | convolution fusion | flops 1343488000 | bytes 10748032 | tf_op jit(solution)/shard_map/bwj,jc->bwc/dot_general | solution.py:36
  18.0 0.1 slice_convert_fusion.6
  18.1 0.0 copy-start.3
  18.1 24.3 %copy.19 = bf16[32,160,1024]{1,0,2:T(8,128)(2,1)} copy(bf16[32,160,1024]{2,1,0:T(8,128)(2,1)} %fusion.8) | data formatting | bytes 20971520 | tf_op jit(solution)/shard_map/bwj,jc->bwc/dot_general | solution.py:36
  42.4 0.0 collective-permute-done
  42.5 0.7 maximum_convert_fusion
  43.1 3.9 %fusion.2 = f32[383,3,1024]{2,0,1:T(8,128)S(1)} fusion(f32[389,3,1024]{2,0,1:T(8,128)S(1)} %maximum_convert_fusion, f32[3,1024]{1,0:T(4,128)S(1)} %get-tuple-element.16, f32[3,1024]{1,0:T(4,128)S(1)} %get-tuple-element.17, f32[3,1024]{1,0:T(4,128)S(1)} %get-tuple-element.18, f32[3,1024]{1,0:T(4,128)S(1)} %get-tuple-element.19, ...), kind=kLoop, calls=%fused_computation.3 | loop fusion | flops 15295488 | bytes 37736448 | tf_op jit(solution)/shard_map/add | solution.py:21
  47.0 0.2 fusion.12
  47.3 1.5 fusion.24
  48.7 1.6 fusion.19
  50.3 2.5 %copy.14 = bf16[8,32,1024]{1,0,2:T(8,128)(2,1)S(1)} copy(bf16[8,32,1024]{2,1,0:T(8,128)(2,1)} %bitcast.46) | data formatting | bytes 1048576 | tf_op jit(solution)/shard_map/slice | solution.py:31
  52.8 3.4 %copy.15 = bf16[8,32,1024]{1,0,2:T(8,128)(2,1)} copy(bf16[8,32,1024]{2,1,0:T(8,128)(2,1)} %bitcast.45) | data formatting | bytes 1048576 | tf_op jit(solution)/shard_map/slice | solution.py:31
  56.2 3.4 %copy.16 = bf16[8,32,1024]{1,0,2:T(8,128)(2,1)} copy(bf16[8,32,1024]{2,1,0:T(8,128)(2,1)} %bitcast.44) | data formatting | bytes 1048576 | tf_op jit(solution)/shard_map/slice | solution.py:31
  59.6 3.4 %copy.17 = bf16[8,32,1024]{1,0,2:T(8,128)(2,1)} copy(bf16[8,32,1024]{2,1,0:T(8,128)(2,1)} %bitcast.43) | data formatting | bytes 1048576 | tf_op jit(solution)/shard_map/slice | solution.py:31
  63.0 2.0 pad_slice_fusion
  64.9 3.4 %copy.13 = bf16[8,32,1024]{1,0,2:T(8,128)(2,1)} copy(bf16[8,32,1024]{2,1,0:T(8,128)(2,1)} %bitcast.42) | data formatting | bytes 1048576 | tf_op jit(solution)/shard_map/slice | solution.py:31
  68.3 12.3 %concatenate.11 = bf16[8,160,1024]{1,0,2:T(8,128)(2,1)} concatenate(bf16[8,32,1024]{1,0,2:T(8,128)(2,1)} %copy.13, bf16[8,32,1024]{1,0,2:T(8,128)(2,1)S(1)} %copy.14, bf16[8,32,1024]{1,0,2:T(8,128)(2,1)} %copy.15, bf16[8,32,1024]{1,0,2:T(8,128)(2,1)} %copy.16, bf16[8,32,1024]{1,0,2:T(8,128)(2,1)} %copy.17), dimensions={1} | concatenate | bytes 5242880 | tf_op jit(solution)/shard_map/concatenate | solution.py:31
  80.6 10.7 %fusion.9 = f32[8,32,1024]{1,0,2:T(8,128)} fusion(bf16[8,160,1024]{1,0,2:T(8,128)(2,1)} %concatenate.11, bf16[32,160,1024]{1,0,2:T(8,128)(2,1)} %copy.19), kind=kOutput, calls=%fused_computation.18 | convolution fusion | flops 83886080 | bytes 14155776 | tf_op jit(solution)/shard_map/bwc,awc->abc/dot_general | solution.py:39
  91.3 2.9 %copy.18 = f32[8,32,1024]{2,1,0:T(8,128)S(1)} copy(f32[8,32,1024]{1,0,2:T(8,128)} %fusion.9) | data formatting | bytes 2097152 | tf_op jit(solution)/shard_map/bwc,awc->abc/transpose | solution.py:39
  94.2 2.3 %fusion.16 = bf16[256,1024]{1,0:T(8,128)(2,1)} fusion(f32[383,3,1024]{2,0,1:T(8,128)} %copy-done.2, f32[8,32,1024]{2,1,0:T(8,128)S(1)} %copy.18, f32[1024]{0:T(1024)S(1)} %copy-done.5, bf16[383,1,1024]{2,0,1:T(8,128)(2,1)S(1)} %fusion.12), kind=kLoop, calls=%fused_computation.26 | loop fusion | flops 1310720 | bytes 3149824 | tf_op jit(solution)/shard_map/convert_element_type | solution.py:57
  96.5 0.0 all-gather.3.cloned.1.call-update
  96.6 0.0 all-gather.5.cloned.1.call-start
  96.6 0.7 all-gather.5.cloned.1.call-update
  97.3 45.1 %all-gather.3.cloned.1.call-done = bf16[256,4096]{1,0:T(8,128)(2,1)} async-done(((bf16[256,1024]{1,0:T(8,128)(2,1)}), bf16[256,4096]{1,0:T(8,128)(2,1)}) %all-gather.3.cloned.1.call-update) | async-done | bytes 2097168 | tf_op jit(solution)/shard_map/all_gather | solution.py:58
  142.4 55.5 %all-gather.5.cloned.1.call-done = bf16[4096,1024]{1,0:T(8,128)(2,1)} async-done(((bf16[512,1024]{1,0:T(8,128)(2,1)}), bf16[4096,1024]{1,0:T(8,128)(2,1)}) %all-gather.5.cloned.1.call-update) | async-done | bytes 8388624 | tf_op jit(solution)/shard_map/all_gather | solution.py:61
  197.9 7.2 %fusion.14 = bf16[256,1024]{1,0:T(8,128)(2,1)} fusion(bf16[256,4096]{1,0:T(8,128)(2,1)} %all-gather.3.cloned.1.call-done, bf16[4096,1024]{1,0:T(8,128)(2,1)} %all-gather.5.cloned.1.call-done, bf16[256,1024]{1,0:T(8,128)(2,1)S(1)} %copy-done.6), kind=kOutput, calls=%fused_computation.23 | convolution fusion | flops 2148270080 | bytes 11534336 | tf_op jit(solution)/shard_map/dot_general | solution.py:59
  (15 shorter events, 0.1 us)
Async XLA Ops:
  6.5 5.9 %copy-start = (bf16[128,1024]{1,0:T(8,128)(2,1)S(1)}, bf16[128,1024]{1,0:T(8,128)(2,1)}, u32[]{:S(2)}) copy-start(bf16[128,1024]{1,0:T(8,128)(2,1)} %param.9) | copy-start | bytes 786436
  6.5 135.9 %all-gather.3.cloned.1.call-start = ((), (), s32[]{:S(2)}) async-start(), calls=%async_computation | async-start | bytes 2621440 | tf_op jit(solution)/shard_map/all_gather | solution.py:58
  8.0 34.5 %collective-permute-start = (bf16[133,3,1024]{2,0,1:T(8,128)(2,1)S(1)}, bf16[133,3,1024]{2,0,1:T(8,128)(2,1)S(1)}, u32[]{:S(2)}, u32[]{:S(2)}) collective-permute-start(bf16[133,3,1024]{2,0,1:T(8,128)(2,1)S(1)} %slice.94), channel_id=1, source_target_pairs={{0,4},{4,8},{8,12},{12,16},{16,20},{20,24},{24,28},{1,5},{5,9},{9,... | collective-permute-start | bytes 2451464 | tf_op jit(solution)/shard_map/ppermute | solution.py:12
  12.5 5.5 %copy-start.4 = (bf16[7,3,1024]{2,0,1:T(8,128)(2,1)S(1)}, bf16[7,3,1024]{2,0,1:T(8,128)(2,1)}, u32[]{:S(2)}) copy-start(bf16[7,3,1024]{2,0,1:T(8,128)(2,1)} %param.8) | copy-start | bytes 129028
  18.1 24.4 %copy-start.3 = (bf16[256,3,1024]{2,0,1:T(8,128)(2,1)S(1)}, bf16[256,3,1024]{2,0,1:T(8,128)(2,1)}, u32[]{:S(2)}) copy-start(bf16[256,3,1024]{2,0,1:T(8,128)(2,1)} %param.7) | copy-start | bytes 4718596
  47.0 3.2 %copy-start.2 = (f32[383,3,1024]{2,0,1:T(8,128)}, f32[383,3,1024]{2,0,1:T(8,128)S(1)}, u32[]{:S(2)}) copy-start(f32[383,3,1024]{2,0,1:T(8,128)S(1)} %fusion.2) | copy-start | bytes 14118916
  91.3 2.9 %copy-start.5 = (f32[1024]{0:T(1024)S(1)}, f32[1024]{0:T(1024)}, u32[]{:S(2)}) copy-start(f32[1024]{0:T(1024)} %param.10) | copy-start | bytes 12292
  91.3 106.6 %copy-start.6 = (bf16[256,1024]{1,0:T(8,128)(2,1)S(1)}, bf16[256,1024]{1,0:T(8,128)(2,1)}, u32[]{:S(2)}) copy-start(bf16[256,1024]{1,0:T(8,128)(2,1)} %param.6) | copy-start | bytes 1572868
  96.6 101.3 %all-gather.5.cloned.1.call-start = ((), (), s32[]{:S(2)}) async-start(), calls=%async_computation.1 | async-start | bytes 9437184 | tf_op jit(solution)/shard_map/all_gather | solution.py:61
  197.9 7.2 %copy-start.1 = (bf16[128,1024]{1,0:T(8,128)(2,1)S(1)}, bf16[128,1024]{1,0:T(8,128)(2,1)}, u32[]{:S(2)}) copy-start(bf16[128,1024]{1,0:T(8,128)(2,1)} %param.9) | copy-start | bytes 786436
Sparse Core Ops, SparseCore 0:
  96.7 45.6 all-gather.2
  144.3 53.5 all-gather.4
where the time goes:
time: 213 us; the launch traced here: 212 us
  waiting for transfers between devices  101 us (47%)
  local copies, waits for them, and re-layouts  60.5 us (28%)
  matrix products  23.4 us (11%)
  between operations  13.6 us (6%)
  other arithmetic  8.61 us (4%)
  starting transfers between devices  4.55 us (2%)
    all_gather x1, waiting for transfers between devices, on_device(): lax.all_gather(out_weight, 'ctx', axis=0, tiled=True)  55.5 us
    all_gather x1, waiting for transfers between devices, on_device(): whole = lax.all_gather(gated, 'tp', axis=1, tiled=True)  45.1 us
    dot_general x1, local copies, waits for them, and re-layouts, medium_mix(): jnp.einsum('bwj,jc->bwc', select, medium_filter, preferred_element_type=j...  24.3 us
    slice x7, local copies, waits for them, and re-layouts, medium_mix(): blocks[i:i + nblocks]  19.6 us
    concatenate x1, local copies, waits for them, and re-layouts, medium_mix(): jnp.concatenate([blocks[i:i + nblocks] for i in range(reach // BLOCK + 1)...  12.3 us
    dot_general x1, matrix products, medium_mix(): jnp.einsum('bwc,awc->abc', banded, windows, preferred_element_type=jnp.fl...  10.7 us
    dot_general x1, matrix products, on_device(): jnp.dot(whole, lax.all_gather(out_weight, 'ctx', axis=0, tiled=True), pre...  7.18 us
    dot_general x1, matrix products, medium_mix(): jnp.einsum('bwj,jc->bwc', select, medium_filter, preferred_element_type=j...  5.5 us
  transfers between devices with their start and end apart: 3, of which 2 were waited for; matrix products, arithmetic and copies ran while one was open for 14% of the time, Pallas kernels for 0%

commit v1 on v0

v1 whole, which is shorter than its diff:
```python
import functools

import jax
import jax.numpy as jnp
import numpy as np
from jax import lax
from jax.experimental import pallas as pl
from jax.experimental.pallas import tpu as pltpu
from jax.sharding import PartitionSpec as P

WIDE = 256
STEP = 128
EDGE = 16
MESH = pl.DeviceIdType.MESH


def spectrum_tables(length, reach):
    half = length // 2
    angle = 2 * np.pi / length * np.outer(np.arange(half) + 0.5, np.arange(length))
    forward = np.concatenate([np.cos(angle), np.sin(angle)], 0)
    inverse = (2.0 / length) * forward.T[reach:]

    def two(table):
        high = table.astype(np.float32).astype(jnp.bfloat16)
        return high, (table - high.astype(np.float64)).astype(np.float32).astype(jnp.bfloat16)

    return two(forward) + two(inverse)


def dot(a, b):
    return jnp.dot(a, b, preferred_element_type=jnp.float32)


def kernel(
    n_ctx, n_tp, taps,
    residual, proj, short, medium, skip, weight, fwd_hi, fwd_lo, inv_hi, inv_lo,
    out,
    whole, gated, total, wide, short32, product, transfer, query, spec, spec_hi, spec_lo, edge,
    own_sem, w_send, w_recv, z_send, z_recv, edge_send, edge_recv, tail_send, tail_recv,
):
    rows, chans = residual.shape[0], proj.shape[2]
    depth, outs = weight.shape
    reach = medium.shape[0]
    chunks = chans // WIDE
    length = rows + reach
    half = length // 2
    me, z = lax.axis_index("ctx"), lax.axis_index("tp")
    after, before = lax.rem(me + 1, n_ctx), lax.rem(me + n_ctx - 1, n_ctx)
    square = n_ctx == 8 and n_tp == 4 and chans == 2 * depth

    def flip(bit):
        return me + bit - 2 * bit * lax.rem(me // bit, 2)

    if square:
        core, side, up = flip(1), flip(2), flip(4)
        corner = side + up - me

    barrier = pltpu.get_barrier_semaphore()

    def greet(where):
        pl.semaphore_signal(barrier, inc=1, device_id=where, device_id_type=MESH)

    if square:
        for peer in (core, side, up, after, before):
            greet({"ctx": peer})
        greeted = 5
    else:
        @pl.loop(1, n_ctx)
        def _(by):
            greet({"ctx": lax.rem(me + by, n_ctx)})
        greeted = n_ctx - 1

    @pl.when(z < n_tp - 1)
    def _():
        greet({"tp": z + 1})

    @pl.when(z > 0)
    def _():
        greet({"tp": z - 1})

    def columns(q):
        return pl.ds(pl.multiple_of(q * WIDE, WIDE), WIDE)

    def edge_copy():
        return pltpu.make_async_remote_copy(
            src_ref=proj.at[:, pl.ds(rows - EDGE, EDGE), :], dst_ref=edge,
            send_sem=edge_send, recv_sem=edge_recv, device_id={"ctx": after}, device_id_type=MESH)

    def tail_copy(q):
        return pltpu.make_async_remote_copy(
            src_ref=product.at[pl.ds(rows, reach), columns(q)],
            dst_ref=product.at[pl.ds(0, reach), columns(q)],
            send_sem=tail_send.at[q], recv_sem=tail_recv.at[q],
            device_id={"ctx": after}, device_id_type=MESH)

    def z_copy(way, step, q, origin):
        return pltpu.make_async_remote_copy(
            src_ref=gated.at[origin, q], dst_ref=gated.at[origin, q],
            send_sem=z_send.at[way, step, q], recv_sem=z_recv.at[way, step, q],
            device_id={"tp": z + 1 if way == 0 else z - 1}, device_id_type=MESH)

    def z_sends(step, q, act):
        @pl.when((z < n_tp - 1) & (z >= step))
        def _():
            act(z_copy(0, step, q, z - step))

        @pl.when((z > 0) & (z + step <= n_tp - 1))
        def _():
            act(z_copy(1, step, q, z + step))

    def z_wait(step, q):
        @pl.when(z - 1 - step >= 0)
        def _():
            z_copy(0, step, q, z - 1 - step).wait_recv()

        @pl.when(z + 1 + step <= n_tp - 1)
        def _():
            z_copy(1, step, q, z + 1 + step).wait_recv()

    def z_pass(step, q):
        z_wait(step, q)
        if step + 1 < n_tp - 1:
            z_sends(step + 1, q, lambda copy: copy.start())

    part = depth // 2

    def w_rows(block, h):
        return pl.ds(pl.multiple_of(block * depth + h * part, part), part)

    def w_copy(slot, block, h, to, own=False):
        return pltpu.make_async_remote_copy(
            src_ref=weight.at[pl.ds(h * part, part), :] if own else whole.at[w_rows(block, h), :],
            dst_ref=whole.at[w_rows(block, h), :],
            send_sem=w_send.at[slot], recv_sem=w_recv.at[slot],
            device_id={"ctx": to}, device_id_type=MESH)

    def w_all(by):
        return pltpu.make_async_remote_copy(
            src_ref=weight, dst_ref=whole.at[pl.ds(pl.multiple_of(me * depth, depth), depth), :],
            send_sem=w_send.at[by], recv_sem=w_recv.at[by],
            device_id={"ctx": lax.rem(me + by, n_ctx)}, device_id_type=MESH)

    own = pltpu.make_async_copy(
        weight, whole.at[pl.ds(pl.multiple_of(me * depth, depth), depth), :], own_sem)

    def mixed(stream, start, cols):
        acc = None
        for j in range(taps):
            term = short32[stream, j : j + 1, cols] * wide[stream, pl.ds(EDGE + start - j, STEP), cols]
            acc = term if acc is None else acc + term
        return acc

    def multiply(start, cols):
        product[pl.ds(reach + start, STEP), cols] = (
            mixed(1, start, cols) * mixed(2, start, cols)
        ).astype(jnp.bfloat16)

    for stream in range(3):
        short32[stream, 0:taps, :] = short[stream].astype(jnp.float32)

    @pl.loop(0, chunks)
    def _(q):
        cols = columns(q)
        for stream in range(3):
            wide[stream, pl.ds(EDGE, rows), cols] = proj[stream, :, cols].astype(jnp.float32)

    pl.semaphore_wait(barrier, greeted + jnp.where(z < n_tp - 1, 1, 0) + jnp.where(z > 0, 1, 0))
    edge_copy().start()

    @pl.loop(0, chunks)
    def _(q):
        for start in range(rows - reach, rows, STEP):
            multiply(start, columns(q))
        tail_copy(q).start()

    own.start()
    sent = []
    if square:
        for slot, h, to in ((0, 0, side), (1, 1, up), (2, 1, side), (3, 0, up), (4, 0, core), (5, 1, core)):
            sent.append(w_copy(slot, me, h, to, own=True))
            sent[-1].start()
    else:
        @pl.loop(1, n_ctx)
        def _(by):
            w_all(by).start()

    @pl.loop(0, chunks)
    def _(q):
        taps_now = medium[:, columns(q)]
        transfer[:, columns(q)] = dot(fwd_hi[:, 0:reach], taps_now) + dot(fwd_lo[:, 0:reach], taps_now)

    edge_copy().wait_recv()
    for stream in range(3):
        wide[stream, 0:EDGE, :] = jnp.where(me > 0, edge[stream].astype(jnp.float32), 0.0)

    @pl.loop(0, chunks)
    def _(q):
        cols = columns(q)
        for start in range(0, rows - reach, STEP):
            multiply(start, cols)
        for start in range(0, rows, STEP):
            query[pl.ds(start, STEP), :] = mixed(0, start, cols)
        tail_copy(q).wait_recv()

        @pl.when(me == 0)
        def _():
            product[0:reach, cols] = jnp.zeros((reach, WIDE), jnp.bfloat16)

        window = product[:, cols]
        spec[...] = dot(fwd_hi[...], window) + dot(fwd_lo[...], window)
        for top in range(0, half, 64):
            a, b = spec[top : top + 64, :], spec[half + top : half + top + 64, :]
            c, d = transfer[top : top + 64, cols], transfer[half + top : half + top + 64, cols]
            for at, value in ((top, a * c - b * d), (half + top, a * d + b * c)):
                high = value.astype(jnp.bfloat16)
                spec_hi[at : at + 64, :] = high
                spec_lo[at : at + 64, :] = (value - high.astype(jnp.float32)).astype(jnp.bfloat16)
        filtered = dot(inv_hi[...], spec_hi[...]) + dot(inv_hi[...], spec_lo[...]) + dot(inv_lo[...], spec_hi[...])
        filtered = filtered + skip[:, cols] * product[pl.ds(reach, rows), cols].astype(jnp.float32)
        gated[z, q] = (query[...] * filtered).astype(jnp.bfloat16)
        z_sends(0, q, lambda copy: copy.start())

        @pl.when(q >= 1)
        def _():
            z_pass(0, q - 1)

    def project(origin, first, count):
        @pl.loop(0, outs // WIDE)
        def _(tile):
            cols = columns(tile)
            acc = total[:, cols]
            for q in range(first, first + count):
                at = pl.multiple_of(origin * chans + q * WIDE, WIDE)
                acc = acc + dot(gated[origin, q], whole[pl.ds(at, WIDE), cols])
            total[:, cols] = acc

    total[...] = residual[...].astype(jnp.float32)

    def near(origin):
        return (origin - z <= n_tp - 2) & (z - origin <= n_tp - 2)

    if square:
        far = corner // 2

        def arrived(slot, block, h):
            w_copy(slot, block, h, core).wait_recv()

        def relay(slot, block, h, to):
            copy = w_copy(slot, block, h, to)
            copy.start()
            sent.append(copy)

        arrived(0, side, 0)
        relay(6, side, 0, up)
        relay(8, side, 0, core)
        arrived(1, up, 1)
        relay(7, up, 1, side)
        relay(9, up, 1, core)
        z_pass(0, chunks - 1)
        for q in range(chunks - 1):
            z_pass(1, q)
        arrived(2, side, 1)
        relay(10, side, 1, core)
        arrived(3, up, 0)
        relay(11, up, 0, core)
        z_pass(1, chunks - 1)
        own.wait()
        for slot, block, h in ((4, core, 0), (5, core, 1)):
            arrived(slot, block, h)
        other = core - me
        for slot, block, h in ((8, side, 0), (9, up, 1), (10, side, 1), (11, up, 0)):
            arrived(slot, block + other, h)

        @pl.loop(0, n_tp)
        def _(origin):
            @pl.when(near(origin) & (origin != far))
            def _():
                project(origin, 0, chunks)

        arrived(6, corner, 0)
        relay(12, corner, 0, core)
        arrived(7, corner, 1)
        relay(13, corner, 1, core)
        arrived(12, corner + other, 0)
        arrived(13, corner + other, 1)

        @pl.when(near(far))
        def _():
            project(far, 0, chunks)
    else:
        z_pass(0, chunks - 1)
        for step in range(1, n_tp - 2):
            @pl.loop(0, chunks)
            def _(q):
                z_pass(step, q)
        own.wait()

        @pl.loop(1, n_ctx)
        def _(by):
            w_all(by).wait_recv()

        @pl.loop(0, n_tp)
        def _(origin):
            @pl.when(near(origin))
            def _():
                project(origin, 0, chunks)

    for q in range(chunks):
        z_wait(n_tp - 2, q)

        @pl.when((z == 0) | (z == n_tp - 1))
        def _():
            project(n_tp - 1 - z, q, 1)

    out[...] = total[...].astype(jnp.bfloat16)

    edge_copy().wait_send()
    for q in range(chunks):
        tail_copy(q).wait_send()
    if square:
        for copy in sent:
            copy.wait_send()
    else:
        @pl.loop(1, n_ctx)
        def _(by):
            w_all(by).wait_send()
    for step in range(n_tp - 1):
        @pl.loop(0, chunks)
        def _(q):
            z_sends(step, q, lambda copy: copy.wait_send())


def on_device(n_ctx, n_tp, residual, proj, short_filter, medium_filter, skip, out_weight):
    rows, _, chans = proj.shape
    depth, outs = out_weight.shape
    taps, reach = short_filter.shape[0], medium_filter.shape[0]
    length, chunks = rows + reach, chans // WIDE
    tables = [jnp.asarray(table) for table in spectrum_tables(length, reach)]
    in_vmem = pl.BlockSpec(memory_space=pltpu.VMEM)
    dma = pltpu.SemaphoreType.DMA
    return pl.pallas_call(
        functools.partial(kernel, n_ctx, n_tp, taps),
        out_shape=jax.ShapeDtypeStruct((rows, outs), jnp.bfloat16),
        in_specs=[in_vmem] * 5 + [pl.BlockSpec(memory_space=pl.ANY)] + [in_vmem] * 4,
        out_specs=in_vmem,
        scratch_shapes=[
            pltpu.VMEM((n_ctx * depth, outs), jnp.bfloat16),
            pltpu.VMEM((n_tp, chunks, rows, WIDE), jnp.bfloat16),
            pltpu.VMEM((rows, outs), jnp.float32),
            pltpu.VMEM((3, EDGE + rows, chans), jnp.float32),
            pltpu.VMEM((3, 8, chans), jnp.float32),
            pltpu.VMEM((length, chans), jnp.bfloat16),
            pltpu.VMEM((length, chans), jnp.float32),
            pltpu.VMEM((rows, WIDE), jnp.float32),
            pltpu.VMEM((length, WIDE), jnp.float32),
            pltpu.VMEM((length, WIDE), jnp.bfloat16),
            pltpu.VMEM((length, WIDE), jnp.bfloat16),
            pltpu.VMEM((3, EDGE, chans), jnp.bfloat16),
            dma,
            dma((max(n_ctx, 14),)),
            dma((max(n_ctx, 14),)),
            dma((2, n_tp - 1, chunks)),
            dma((2, n_tp - 1, chunks)),
            dma,
            dma,
            dma((chunks,)),
            dma((chunks,)),
        ],
        compiler_params=pltpu.CompilerParams(
            collective_id=0, has_side_effects=True, vmem_limit_bytes=48 * 2**20
        ),
        cost_estimate=pl.CostEstimate(
            flops=2 * rows * n_ctx * depth * outs, bytes_accessed=2 * rows * chans * 5, transcendentals=0
        ),
    )(
        residual, proj.transpose(1, 0, 2), short_filter.transpose(1, 0, 2), medium_filter,
        skip.reshape(1, chans), out_weight, *tables,
    )


def solution(mesh):
    in_specs = (
        P("ctx", "tp"),
        P("ctx", None, "tp"),
        P(None, None, "tp"),
        P(None, "tp"),
        P("tp"),
        P("ctx", "tp"),
    )
    return jax.shard_map(
        functools.partial(on_device, mesh.shape["ctx"], mesh.shape["tp"]),
        mesh=mesh, in_specs=in_specs, out_specs=P("ctx", "tp"), check_vma=False,
    )
```

time: 213 us -> 60.9 us (0.29)
  waiting for transfers between devices: 101 us -> 0 us
  Pallas kernels: 0 us -> 49.8 us
  local copies, waits for them, and re-layouts: 60.5 us -> 10.7 us
  matrix products: 23.4 us -> 0 us
  between operations: 13.6 us -> 0.02 us
  other arithmetic: 8.61 us -> 0 us
  starting transfers between devices: 4.55 us -> 0 us
    all_gather x2 -> x0, waiting for transfers between devices: 101 us -> none  [the longest x1 55.5 us: on_device(): lax.all_gather(out_weight, 'ctx', axis=0, tiled=True)]
    pallas_call x0 -> x1, Pallas kernels: none -> 49.8 us  [on_device(): pl.pallas_call(functools.partial(kernel, n_ctx, n_tp, taps), out_shape=ja...]
    dot_general x1 -> x0, local copies, waits for them, and re-layouts: 24.3 us -> none  [medium_mix(): jnp.einsum('bwj,jc->bwc', select, medium_filter, preferred_element_type=j...]
    dot_general x3 -> x0, matrix products: 23.4 us -> none  [the longest x1 10.7 us: medium_mix(): jnp.einsum('bwc,awc->abc', banded, windows, preferred_element_type=jnp.fl...]
    slice x8 -> x0, local copies, waits for them, and re-layouts: 21 us -> none  [the longest x7 19.6 us: medium_mix(): blocks[i:i + nblocks]]
    concatenate x1 -> x0, local copies, waits for them, and re-layouts: 12.3 us -> none  [medium_mix(): jnp.concatenate([blocks[i:i + nblocks] for i in range(reach // BLOCK + 1)...]
    unnamed x18 -> x21, local copies, waits for them, and re-layouts: 0.07 us -> 10.7 us
    convert_element_type x4 -> x0, other arithmetic: 4.68 us -> none  [the longest x1 2.33 us: on_device(): gated = (query * filtered).astype(jnp.bfloat16)]
  transfers between devices with their start and end apart: 3 -> 0, of which waited for: 2 -> 0; matrix products, arithmetic and copies ran while one was open for 14% -> 0% of each run, Pallas kernels for 0% -> 0%
where the time goes in v1:
time: 60.9 us; the launch traced here: 60.5 us
  Pallas kernels  49.8 us (82%)
  local copies, waits for them, and re-layouts  10.7 us (18%)
    pallas_call x1, Pallas kernels, on_device(): pl.pallas_call(functools.partial(kernel, n_ctx, n_tp, taps), out_shape=ja...  49.8 us
    unnamed x21, local copies, waits for them, and re-layouts  10.7 us

profile of v1, /device:TPU:1, one launch (start us, length us, event | category | flops | bytes accessed | tf_op | source)
XLA Modules:
  0.0 60.5 jit_solution(13166539001227414259)
XLA Ops:
  0.0 0.0 copy-start
  0.0 1.4 %copy-done = bf16[256,3,1024]{2,0,1:T(8,128)(2,1)S(1)} copy-done((bf16[256,3,1024]{2,0,1:T(8,128)(2,1)S(1)}, bf16[256,3,1024]{2,0,1:T(8,128)(2,1)}, u32[]{:S(2)}) %copy-start) | copy-done | bytes 1572888
  1.4 0.0 copy-start.1
  1.4 1.2 %copy-done.1 = bf16[512,1024]{1,0:T(8,128)(2,1)S(1)} copy-done((bf16[512,1024]{1,0:T(8,128)(2,1)S(1)}, bf16[512,1024]{1,0:T(8,128)(2,1)}, u32[]{:S(2)}) %copy-start.1) | copy-done | bytes 1048600
  2.6 0.0 copy-start.2
  2.6 1.0 %copy-done.2 = bf16[256,1024]{1,0:T(8,128)(2,1)S(1)} copy-done((bf16[256,1024]{1,0:T(8,128)(2,1)S(1)}, bf16[256,1024]{1,0:T(8,128)(2,1)}, u32[]{:S(2)}) %copy-start.2) | copy-done | bytes 524312
  3.7 0.0 copy-start.3
  3.7 0.9 %copy-done.3 = bf16[128,1024]{1,0:T(8,128)(2,1)S(1)} copy-done((bf16[128,1024]{1,0:T(8,128)(2,1)S(1)}, bf16[128,1024]{1,0:T(8,128)(2,1)}, u32[]{:S(2)}) %copy-start.3) | copy-done | bytes 262168
  4.6 0.0 copy-start.4
  4.6 0.8 %copy-done.4 = bf16[7,3,1024]{2,0,1:T(8,128)(2,1)S(1)} copy-done((bf16[7,3,1024]{2,0,1:T(8,128)(2,1)S(1)}, bf16[7,3,1024]{2,0,1:T(8,128)(2,1)}, u32[]{:S(2)}) %copy-start.4) | copy-done | bytes 43032
  5.4 0.0 copy-start.5
  5.4 0.7 %copy-done.5 = f32[1024]{0:T(1024)S(1)} copy-done((f32[1024]{0:T(1024)S(1)}, f32[1024]{0:T(1024)}, u32[]{:S(2)}) %copy-start.5) | copy-done | bytes 4120
  6.1 0.0 copy-start.6
  6.1 1.0 %copy-done.6 = bf16[384,384]{1,0:T(8,128)(2,1)S(1)} copy-done((bf16[384,384]{1,0:T(8,128)(2,1)S(1)}, bf16[384,384]{1,0:T(8,128)(2,1)}, u32[]{:S(2)}) %copy-start.6) | copy-done | bytes 294936
  7.1 0.0 copy-start.7
  7.1 1.0 %copy-done.7 = bf16[384,384]{1,0:T(8,128)(2,1)S(1)} copy-done((bf16[384,384]{1,0:T(8,128)(2,1)S(1)}, bf16[384,384]{1,0:T(8,128)(2,1)}, u32[]{:S(2)}) %copy-start.7) | copy-done | bytes 294936
  8.0 0.0 copy-start.8
  8.0 0.9 %copy-done.8 = bf16[256,384]{1,0:T(8,128)(2,1)S(1)} copy-done((bf16[256,384]{1,0:T(8,128)(2,1)S(1)}, bf16[256,384]{1,0:T(8,128)(2,1)}, u32[]{:S(2)}) %copy-start.8) | copy-done | bytes 196632
  9.0 0.0 copy-start.9
  9.0 0.9 %copy-done.9 = bf16[256,384]{1,0:T(8,128)(2,1)S(1)} copy-done((bf16[256,384]{1,0:T(8,128)(2,1)S(1)}, bf16[256,384]{1,0:T(8,128)(2,1)}, u32[]{:S(2)}) %copy-start.9) | copy-done | bytes 196632
  9.9 49.8 %shard_map.100 = bf16[256,1024]{1,0:T(8,128)(2,1)S(1)} custom-call(bf16[256,1024]{1,0:T(8,128)(2,1)S(1)} %copy-done.2, bf16[3,256,1024]{2,1,0:T(8,128)(2,1)S(1)} %bitcast.3, bf16[3,7,1024]{2,1,0:T(8,128)(2,1)S(1)} %bitcast.4, bf16[128,1024]{1,0:T(8,128)(2,1)S(1)} %copy-done.3, f32[1,1024]{1,0:T(1,128)S(1)} %bitcast.5, bf16[512,1024]{1,0:T(8,128)(2,1)S(1)} %copy-done.1, ...), custom_call_target="tpu_custom_call" | custom-call | flops 2147483648 | bytes 2621440 | tf_op jit(solution)/shard_map/pallas_call | solution.py:341
  59.7 0.8 %copy.12 = bf16[256,1024]{1,0:T(8,128)(2,1)} copy(bf16[256,1024]{1,0:T(8,128)(2,1)S(1)} %shard_map.100) | data formatting | bytes 1048576
Async XLA Ops:
  0.0 1.4 %copy-start = (bf16[256,3,1024]{2,0,1:T(8,128)(2,1)S(1)}, bf16[256,3,1024]{2,0,1:T(8,128)(2,1)}, u32[]{:S(2)}) copy-start(bf16[256,3,1024]{2,0,1:T(8,128)(2,1)} %param.11) | copy-start | bytes 4718596
  1.4 1.2 %copy-start.1 = (bf16[512,1024]{1,0:T(8,128)(2,1)S(1)}, bf16[512,1024]{1,0:T(8,128)(2,1)}, u32[]{:S(2)}) copy-start(bf16[512,1024]{1,0:T(8,128)(2,1)} %weight.1) | copy-start | bytes 3145732
  2.6 1.0 %copy-start.2 = (bf16[256,1024]{1,0:T(8,128)(2,1)S(1)}, bf16[256,1024]{1,0:T(8,128)(2,1)}, u32[]{:S(2)}) copy-start(bf16[256,1024]{1,0:T(8,128)(2,1)} %residual.1) | copy-start | bytes 1572868
  3.7 0.9 %copy-start.3 = (bf16[128,1024]{1,0:T(8,128)(2,1)S(1)}, bf16[128,1024]{1,0:T(8,128)(2,1)}, u32[]{:S(2)}) copy-start(bf16[128,1024]{1,0:T(8,128)(2,1)} %medium.1) | copy-start | bytes 786436
  4.6 0.8 %copy-start.4 = (bf16[7,3,1024]{2,0,1:T(8,128)(2,1)S(1)}, bf16[7,3,1024]{2,0,1:T(8,128)(2,1)}, u32[]{:S(2)}) copy-start(bf16[7,3,1024]{2,0,1:T(8,128)(2,1)} %param.12) | copy-start | bytes 129028
  5.4 0.7 %copy-start.5 = (f32[1024]{0:T(1024)S(1)}, f32[1024]{0:T(1024)}, u32[]{:S(2)}) copy-start(f32[1024]{0:T(1024)} %param.14) | copy-start | bytes 12292
  6.1 1.0 %copy-start.6 = (bf16[384,384]{1,0:T(8,128)(2,1)S(1)}, bf16[384,384]{1,0:T(8,128)(2,1)}, u32[]{:S(2)}) copy-start(bf16[384,384]{1,0:T(8,128)(2,1)} %constant.9.clone.fwd_lo) | copy-start | bytes 884740
  7.1 1.0 %copy-start.7 = (bf16[384,384]{1,0:T(8,128)(2,1)S(1)}, bf16[384,384]{1,0:T(8,128)(2,1)}, u32[]{:S(2)}) copy-start(bf16[384,384]{1,0:T(8,128)(2,1)} %constant.8.clone.fwd_hi) | copy-start | bytes 884740
  8.0 0.9 %copy-start.8 = (bf16[256,384]{1,0:T(8,128)(2,1)S(1)}, bf16[256,384]{1,0:T(8,128)(2,1)}, u32[]{:S(2)}) copy-start(bf16[256,384]{1,0:T(8,128)(2,1)} %constant.11.clone.inv_lo) | copy-start | bytes 589828
  9.0 0.9 %copy-start.9 = (bf16[256,384]{1,0:T(8,128)(2,1)S(1)}, bf16[256,384]{1,0:T(8,128)(2,1)}, u32[]{:S(2)}) copy-start(bf16[256,384]{1,0:T(8,128)(2,1)} %constant.10.clone.inv_hi) | copy-start | bytes 589828

commit v2 on v1

--- a/solution.py
+++ b/solution.py
@@ -20,11 +20,7 @@
     forward = np.concatenate([np.cos(angle), np.sin(angle)], 0)
     inverse = (2.0 / length) * forward.T[reach:]
 
-    def two(table):
-        high = table.astype(np.float32).astype(jnp.bfloat16)
-        return high, (table - high.astype(np.float64)).astype(np.float32).astype(jnp.bfloat16)
-
-    return two(forward) + two(inverse)
+    return np.concatenate([forward, inverse], 0).astype(np.float32)
 
 
 def dot(a, b):
@@ -33,10 +29,12 @@
 
 def kernel(
     n_ctx, n_tp, taps,
-    residual, proj, short, medium, skip, weight, fwd_hi, fwd_lo, inv_hi, inv_lo,
+    residual_hbm, proj_hbm, short_hbm, medium_hbm, skip_hbm, weight,
+    tables_hbm,
     out,
+    residual, proj, short, medium, skip, tables32, tables,
     whole, gated, total, wide, short32, product, transfer, query, spec, spec_hi, spec_lo, edge,
-    own_sem, w_send, w_recv, z_send, z_recv, edge_send, edge_recv, tail_send, tail_recv,
+    local_sem, own_sem, w_send, w_recv, z_send, z_recv, edge_send, edge_recv, tail_send, tail_recv,
 ):
     rows, chans = residual.shape[0], proj.shape[2]
     depth, outs = weight.shape
@@ -78,12 +76,30 @@
     def _():
         greet({"tp": z - 1})
 
+    first = rows - reach
+
+    def bring(n, source, target):
+        copy = pltpu.make_async_copy(source, target, local_sem.at[n])
+        copy.start()
+        return copy
+
+    later = pl.ds(first, reach)
+    get_short = bring(0, short_hbm, short)
+    get_tail = bring(1, proj_hbm.at[1:3, later, :], proj.at[1:3, later, :])
+    get_head = bring(2, proj_hbm.at[1:3, 0:first, :], proj.at[1:3, 0:first, :])
+    get_query = bring(3, proj_hbm.at[0], proj.at[0])
+    get_medium = bring(4, medium_hbm, medium)
+    get_tables = bring(5, tables_hbm, tables32)
+    get_rest = [bring(6, skip_hbm, skip), bring(7, residual_hbm, residual)]
+    fwd_hi, fwd_lo = tables.at[0, 0:length, :], tables.at[1, 0:length, :]
+    inv_hi, inv_lo = tables.at[0, pl.ds(length, rows), :], tables.at[1, pl.ds(length, rows), :]
+
     def columns(q):
         return pl.ds(pl.multiple_of(q * WIDE, WIDE), WIDE)
 
     def edge_copy():
         return pltpu.make_async_remote_copy(
-            src_ref=proj.at[:, pl.ds(rows - EDGE, EDGE), :], dst_ref=edge,
+            src_ref=proj_hbm.at[:, pl.ds(rows - EDGE, EDGE), :], dst_ref=edge,
             send_sem=edge_send, recv_sem=edge_recv, device_id={"ctx": after}, device_id_type=MESH)
 
     def tail_copy(q):
@@ -143,37 +159,60 @@
     own = pltpu.make_async_copy(
         weight, whole.at[pl.ds(pl.multiple_of(me * depth, depth), depth), :], own_sem)
 
-    def mixed(stream, start, cols):
+    def mixed(stream, start, count, cols):
         acc = None
         for j in range(taps):
-            term = short32[stream, j : j + 1, cols] * wide[stream, pl.ds(EDGE + start - j, STEP), cols]
+            term = short32[stream, j : j + 1, cols] * wide[stream, pl.ds(EDGE + start - j, count), cols]
             acc = term if acc is None else acc + term
         return acc
 
-    def multiply(start, cols):
-        product[pl.ds(reach + start, STEP), cols] = (
-            mixed(1, start, cols) * mixed(2, start, cols)
+    def multiply(start, count, cols):
+        product[pl.ds(reach + start, count), cols] = (
+            mixed(1, start, count, cols) * mixed(2, start, count, cols)
         ).astype(jnp.bfloat16)
 
+    def widen(stream, start, count, cols):
+        wide[stream, pl.ds(EDGE + start, count), cols] = proj[stream, pl.ds(start, count), cols].astype(jnp.float32)
+
+    def before_edge(q):
+        cols = columns(q)
+        for stream in (1, 2):
+            widen(stream, 0, first, cols)
+        widen(0, 0, rows, cols)
+        spots = [(EDGE, STEP - EDGE)] + [(start, STEP) for start in range(STEP, rows, STEP)]
+        for start, count in spots:
+            if start < first:
+                multiply(start, count, cols)
+            query[pl.ds(start, count), :] = mixed(0, start, count, cols)
+
+    get_short.wait()
     for stream in range(3):
         short32[stream, 0:taps, :] = short[stream].astype(jnp.float32)
+    get_tail.wait()
+    get_head.wait()
 
     @pl.loop(0, chunks)
     def _(q):
         cols = columns(q)
-        for stream in range(3):
-            wide[stream, pl.ds(EDGE, rows), cols] = proj[stream, :, cols].astype(jnp.float32)
+        for stream in (1, 2):
+            widen(stream, first - EDGE, reach + EDGE, cols)
+        for start in range(first, rows, STEP):
+            multiply(start, STEP, cols)
+
+    get_tables.wait()
+
+    @pl.loop(0, (length + rows) // 64)
+    def _(at):
+        span = pl.ds(pl.multiple_of(at * 64, 64), 64)
+        value = tables32[span, :]
+        high = value.astype(jnp.bfloat16)
+        tables[0, span, :] = high
+        tables[1, span, :] = (value - high.astype(jnp.float32)).astype(jnp.bfloat16)
 
     pl.semaphore_wait(barrier, greeted + jnp.where(z < n_tp - 1, 1, 0) + jnp.where(z > 0, 1, 0))
     edge_copy().start()
-
-    @pl.loop(0, chunks)
-    def _(q):
-        for start in range(rows - reach, rows, STEP):
-            multiply(start, columns(q))
+    for q in range(chunks):
         tail_copy(q).start()
-
-    own.start()
     sent = []
     if square:
         for slot, h, to in ((0, 0, side), (1, 1, up), (2, 1, side), (3, 0, up), (4, 0, core), (5, 1, core)):
@@ -183,12 +222,20 @@
         @pl.loop(1, n_ctx)
         def _(by):
             w_all(by).start()
+    own.start()
+
+    get_query.wait()
+    before_edge(0)
+
+    get_medium.wait()
 
     @pl.loop(0, chunks)
     def _(q):
         taps_now = medium[:, columns(q)]
         transfer[:, columns(q)] = dot(fwd_hi[:, 0:reach], taps_now) + dot(fwd_lo[:, 0:reach], taps_now)
 
+    for copy in get_rest:
+        copy.wait()
     edge_copy().wait_recv()
     for stream in range(3):
         wide[stream, 0:EDGE, :] = jnp.where(me > 0, edge[stream].astype(jnp.float32), 0.0)
@@ -196,10 +243,8 @@
     @pl.loop(0, chunks)
     def _(q):
         cols = columns(q)
-        for start in range(0, rows - reach, STEP):
-            multiply(start, cols)
-        for start in range(0, rows, STEP):
-            query[pl.ds(start, STEP), :] = mixed(0, start, cols)
+        multiply(0, EDGE, cols)
+        query[0:EDGE, :] = mixed(0, 0, EDGE, cols)
         tail_copy(q).wait_recv()
 
         @pl.when(me == 0)
@@ -220,21 +265,23 @@
         gated[z, q] = (query[...] * filtered).astype(jnp.bfloat16)
         z_sends(0, q, lambda copy: copy.start())
 
-        @pl.when(q >= 1)
-        def _():
-            z_pass(0, q - 1)
-
-    def project(origin, first, count):
+        @pl.when(q + 1 < chunks)
+        def _():
+            before_edge(q + 1)
+
+    def project(origin, begin, count):
         @pl.loop(0, outs // WIDE)
         def _(tile):
             cols = columns(tile)
             acc = total[:, cols]
-            for q in range(first, first + count):
+            for q in range(begin, begin + count):
                 at = pl.multiple_of(origin * chans + q * WIDE, WIDE)
                 acc = acc + dot(gated[origin, q], whole[pl.ds(at, WIDE), cols])
             total[:, cols] = acc
 
     total[...] = residual[...].astype(jnp.float32)
+    for q in range(chunks):
+        z_pass(0, q)
 
     def near(origin):
         return (origin - z <= n_tp - 2) & (z - origin <= n_tp - 2)
@@ -256,14 +303,14 @@
         arrived(1, up, 1)
         relay(7, up, 1, side)
         relay(9, up, 1, core)
-        z_pass(0, chunks - 1)
-        for q in range(chunks - 1):
+        for q in range(chunks // 2):
             z_pass(1, q)
         arrived(2, side, 1)
         relay(10, side, 1, core)
         arrived(3, up, 0)
         relay(11, up, 0, core)
-        z_pass(1, chunks - 1)
+        for q in range(chunks // 2, chunks):
+            z_pass(1, q)
         own.wait()
         for slot, block, h in ((4, core, 0), (5, core, 1)):
             arrived(slot, block, h)
@@ -288,7 +335,6 @@
         def _():
             project(far, 0, chunks)
     else:
-        z_pass(0, chunks - 1)
         for step in range(1, n_tp - 2):
             @pl.loop(0, chunks)
             def _(q):
@@ -335,15 +381,21 @@
     depth, outs = out_weight.shape
     taps, reach = short_filter.shape[0], medium_filter.shape[0]
     length, chunks = rows + reach, chans // WIDE
-    tables = [jnp.asarray(table) for table in spectrum_tables(length, reach)]
-    in_vmem = pl.BlockSpec(memory_space=pltpu.VMEM)
+    tables = jnp.asarray(spectrum_tables(length, reach))
     dma = pltpu.SemaphoreType.DMA
     return pl.pallas_call(
         functools.partial(kernel, n_ctx, n_tp, taps),
         out_shape=jax.ShapeDtypeStruct((rows, outs), jnp.bfloat16),
-        in_specs=[in_vmem] * 5 + [pl.BlockSpec(memory_space=pl.ANY)] + [in_vmem] * 4,
-        out_specs=in_vmem,
+        in_specs=[pl.BlockSpec(memory_space=pltpu.HBM)] * 7,
+        out_specs=pl.BlockSpec(memory_space=pltpu.VMEM),
         scratch_shapes=[
+            pltpu.VMEM(residual.shape, residual.dtype),
+            pltpu.VMEM((3, rows, chans), proj.dtype),
+            pltpu.VMEM((3, taps, chans), short_filter.dtype),
+            pltpu.VMEM(medium_filter.shape, medium_filter.dtype),
+            pltpu.VMEM((1, chans), skip.dtype),
+            pltpu.VMEM(tables.shape, jnp.float32),
+            pltpu.VMEM((2,) + tables.shape, jnp.bfloat16),
             pltpu.VMEM((n_ctx * depth, outs), jnp.bfloat16),
             pltpu.VMEM((n_tp, chunks, rows, WIDE), jnp.bfloat16),
             pltpu.VMEM((rows, outs), jnp.float32),
@@ -356,6 +408,7 @@
             pltpu.VMEM((length, WIDE), jnp.bfloat16),
             pltpu.VMEM((length, WIDE), jnp.bfloat16),
             pltpu.VMEM((3, EDGE, chans), jnp.bfloat16),
+            dma((8,)),
             dma,
             dma((max(n_ctx, 14),)),
             dma((max(n_ctx, 14),)),
@@ -367,14 +420,14 @@
             dma((chunks,)),
         ],
         compiler_params=pltpu.CompilerParams(
-            collective_id=0, has_side_effects=True, vmem_limit_bytes=48 * 2**20
+            collective_id=0, has_side_effects=True, vmem_limit_bytes=63 * 2**20
         ),
         cost_estimate=pl.CostEstimate(
             flops=2 * rows * n_ctx * depth * outs, bytes_accessed=2 * rows * chans * 5, transcendentals=0
         ),
     )(
         residual, proj.transpose(1, 0, 2), short_filter.transpose(1, 0, 2), medium_filter,
-        skip.reshape(1, chans), out_weight, *tables,
+        skip.reshape(1, chans), out_weight, tables,
     )
 
 

time: 60.9 us -> 53.7 us (0.88)
  local copies, waits for them, and re-layouts: 10.7 us -> 1.87 us
  Pallas kernels: 49.8 us -> 51.2 us
    unnamed x21 -> x1, local copies, waits for them, and re-layouts: 10.7 us -> 1.87 us
    pallas_call x1, Pallas kernels: 49.8 us -> 51.2 us  [on_device(): pl.pallas_call(functools.partial(kernel, n_ctx, n_tp, taps), out_shape=ja...]
where the time goes in v2:
time: 53.7 us; the launch traced here: 53.1 us
  Pallas kernels  51.2 us (95%)
  local copies, waits for them, and re-layouts  1.87 us (3%)
    pallas_call x1, Pallas kernels, on_device(): pl.pallas_call(functools.partial(kernel, n_ctx, n_tp, taps), out_shape=ja...  51.2 us
    unnamed x1, local copies, waits for them, and re-layouts  1.87 us

profile of v2, /device:TPU:1, one launch (start us, length us, event | category | flops | bytes accessed | tf_op | source)
XLA Modules:
  0.0 53.1 jit_solution(2879023817333842855)
XLA Ops:
  0.0 51.2 %shard_map.73 = bf16[256,1024]{1,0:T(8,128)(2,1)} custom-call(bf16[256,1024]{1,0:T(8,128)(2,1)} %residual_hbm.1, bf16[3,256,1024]{2,1,0:T(8,128)(2,1)} %bitcast.3, bf16[3,7,1024]{2,1,0:T(8,128)(2,1)} %bitcast.4, bf16[128,1024]{1,0:T(8,128)(2,1)} %medium_hbm.1, f32[1,1024]{1,0:T(1,128)} %bitcast.5, bf16[512,1024]{1,0:T(8,128)(2,1)} %weight.1, ...), custom_call_target="tpu_custom_call" | custom-call | flops 2147483648 | bytes 2621440 | tf_op jit(solution)/shard_map/pallas_call | solution.py:386
  51.3 1.9 %copy.9 = bf16[256,1024]{1,0:T(8,128)(2,1)} copy(bf16[256,1024]{1,0:T(8,128)(2,1)} %shard_map.73) | data formatting | bytes 1048576

commit v3 on v2

--- a/solution.py
+++ b/solution.py
@@ -10,6 +10,8 @@
 
 WIDE = 256
 STEP = 128
+PIECES = 8
+WINDOW = 6
 EDGE = 16
 MESH = pl.DeviceIdType.MESH
 
@@ -138,17 +140,46 @@
         if step + 1 < n_tp - 1:
             z_sends(step + 1, q, lambda copy: copy.start())
 
-    part = depth // 2
-
-    def w_rows(block, h):
-        return pl.ds(pl.multiple_of(block * depth + h * part, part), part)
-
-    def w_copy(slot, block, h, to, own=False):
+    part = depth // PIECES
+    to_side = [*range(PIECES)]
+    to_up = to_side[PIECES // 2 :] + to_side[: PIECES // 2]
+    ticks = PIECES + PIECES // 2
+
+    def w_copy(slot, block, piece, to, own=False):
+        rows_there = pl.ds(pl.multiple_of(block * depth + piece * part, part), part)
         return pltpu.make_async_remote_copy(
-            src_ref=weight.at[pl.ds(h * part, part), :] if own else whole.at[w_rows(block, h), :],
-            dst_ref=whole.at[w_rows(block, h), :],
+            src_ref=weight.at[pl.ds(piece * part, part), :] if own else whole.at[rows_there, :],
+            dst_ref=whole.at[rows_there, :],
             send_sem=w_send.at[slot], recv_sem=w_recv.at[slot],
             device_id={"ctx": to}, device_id_type=MESH)
+
+    sent = []
+
+    def launch(copy):
+        copy.start()
+        sent.append(copy)
+
+    def w_tick(t):
+        if t < PIECES:
+            launch(w_copy(t, me, to_side[t], side, own=True))
+            launch(w_copy(ticks + t, me, to_up[t], up, own=True))
+        else:
+            launch(w_copy(t, up, to_up[t - PIECES], side))
+            launch(w_copy(ticks + t, side, to_side[t - PIECES], up))
+
+    def w_come(t):
+        if t < PIECES:
+            return (t, side, to_side[t]), (ticks + t, up, to_up[t])
+        return (t, corner, to_up[t - PIECES]), (ticks + t, corner, to_side[t - PIECES])
+
+    def w_take(t):
+        for slot, block, piece in w_come(t):
+            w_copy(slot, block, piece, side if slot < ticks else up).wait_recv()
+            launch(w_copy(2 * ticks + slot, block, piece, core))
+
+    def w_core(t):
+        for slot, block, piece in w_come(t):
+            w_copy(2 * ticks + slot, block + core - me, piece, core).wait_recv()
 
     def w_all(by):
         return pltpu.make_async_remote_copy(
@@ -213,11 +244,11 @@
     edge_copy().start()
     for q in range(chunks):
         tail_copy(q).start()
-    sent = []
     if square:
-        for slot, h, to in ((0, 0, side), (1, 1, up), (2, 1, side), (3, 0, up), (4, 0, core), (5, 1, core)):
-            sent.append(w_copy(slot, me, h, to, own=True))
-            sent[-1].start()
+        for t in range(WINDOW):
+            w_tick(t)
+        for piece in range(PIECES):
+            launch(w_copy(4 * ticks + piece, me, piece, core, own=True))
     else:
         @pl.loop(1, n_ctx)
         def _(by):
@@ -280,62 +311,39 @@
             total[:, cols] = acc
 
     total[...] = residual[...].astype(jnp.float32)
-    for q in range(chunks):
-        z_pass(0, q)
-
     def near(origin):
         return (origin - z <= n_tp - 2) & (z - origin <= n_tp - 2)
 
     if square:
         far = corner // 2
-
-        def arrived(slot, block, h):
-            w_copy(slot, block, h, core).wait_recv()
-
-        def relay(slot, block, h, to):
-            copy = w_copy(slot, block, h, to)
-            copy.start()
-            sent.append(copy)
-
-        arrived(0, side, 0)
-        relay(6, side, 0, up)
-        relay(8, side, 0, core)
-        arrived(1, up, 1)
-        relay(7, up, 1, side)
-        relay(9, up, 1, core)
-        for q in range(chunks // 2):
-            z_pass(1, q)
-        arrived(2, side, 1)
-        relay(10, side, 1, core)
-        arrived(3, up, 0)
-        relay(11, up, 0, core)
-        for q in range(chunks // 2, chunks):
-            z_pass(1, q)
-        own.wait()
-        for slot, block, h in ((4, core, 0), (5, core, 1)):
-            arrived(slot, block, h)
-        other = core - me
-        for slot, block, h in ((8, side, 0), (9, up, 1), (10, side, 1), (11, up, 0)):
-            arrived(slot, block + other, h)
-
-        @pl.loop(0, n_tp)
-        def _(origin):
-            @pl.when(near(origin) & (origin != far))
-            def _():
-                project(origin, 0, chunks)
-
-        arrived(6, corner, 0)
-        relay(12, corner, 0, core)
-        arrived(7, corner, 1)
-        relay(13, corner, 1, core)
-        arrived(12, corner + other, 0)
-        arrived(13, corner + other, 1)
+        events = [(step, q) for step in range(n_tp - 2) for q in range(chunks)]
+        for t in range(ticks):
+            w_take(t)
+            if t + WINDOW < ticks:
+                w_tick(t + WINDOW)
+            if 1 <= t <= len(events):
+                z_pass(*events[t - 1])
+            if t == len(events):
+                own.wait()
+                for piece in range(PIECES):
+                    w_copy(4 * ticks + piece, core, piece, core).wait_recv()
+                for early in range(PIECES):
+                    w_core(early)
+
+                @pl.loop(0, n_tp)
+                def _(origin):
+                    @pl.when(near(origin) & (origin != far))
+                    def _():
+                        project(origin, 0, chunks)
+
+        for late in range(PIECES, ticks):
+            w_core(late)
 
         @pl.when(near(far))
         def _():
             project(far, 0, chunks)
     else:
-        for step in range(1, n_tp - 2):
+        for step in range(n_tp - 2):
             @pl.loop(0, chunks)
             def _(q):
                 z_pass(step, q)
@@ -410,8 +418,8 @@
             pltpu.VMEM((3, EDGE, chans), jnp.bfloat16),
             dma((8,)),
             dma,
-            dma((max(n_ctx, 14),)),
-            dma((max(n_ctx, 14),)),
+            dma((max(n_ctx, 7 * PIECES),)),
+            dma((max(n_ctx, 7 * PIECES),)),
             dma((2, n_tp - 1, chunks)),
             dma((2, n_tp - 1, chunks)),
             dma,

time: 53.7 us -> 53.2 us (level)
  no operation moved by 1% of the time
where the time goes in v3:
time: 53.2 us; the launch traced here: 52.6 us
  Pallas kernels  50.7 us (95%)
  local copies, waits for them, and re-layouts  1.87 us (4%)
    pallas_call x1, Pallas kernels, on_device(): pl.pallas_call(functools.partial(kernel, n_ctx, n_tp, taps), out_shape=ja...  50.7 us
    unnamed x1, local copies, waits for them, and re-layouts  1.87 us

profile of v3, /device:TPU:1, one launch (start us, length us, event | category | flops | bytes accessed | tf_op | source)
XLA Modules:
  0.0 52.6 jit_solution(5435952148160299678)
XLA Ops:
  0.0 50.7 %shard_map.73 = bf16[256,1024]{1,0:T(8,128)(2,1)} custom-call(bf16[256,1024]{1,0:T(8,128)(2,1)} %residual_hbm.1, bf16[3,256,1024]{2,1,0:T(8,128)(2,1)} %bitcast.3, bf16[3,7,1024]{2,1,0:T(8,128)(2,1)} %bitcast.4, bf16[128,1024]{1,0:T(8,128)(2,1)} %medium_hbm.1, f32[1,1024]{1,0:T(1,128)} %bitcast.5, bf16[512,1024]{1,0:T(8,128)(2,1)} %weight.1, ...), custom_call_target="tpu_custom_call" | custom-call | flops 2147483648 | bytes 2621440 | tf_op jit(solution)/shard_map/pallas_call | solution.py:394
  50.8 1.9 %copy.9 = bf16[256,1024]{1,0:T(8,128)(2,1)} copy(bf16[256,1024]{1,0:T(8,128)(2,1)} %shard_map.73) | data formatting | bytes 1048576

commit v4 on v3

--- a/solution.py
+++ b/solution.py
@@ -222,28 +222,17 @@
     get_tail.wait()
     get_head.wait()
 
-    @pl.loop(0, chunks)
-    def _(q):
+    def tail(q):
         cols = columns(q)
         for stream in (1, 2):
             widen(stream, first - EDGE, reach + EDGE, cols)
         for start in range(first, rows, STEP):
             multiply(start, STEP, cols)
 
-    get_tables.wait()
-
-    @pl.loop(0, (length + rows) // 64)
-    def _(at):
-        span = pl.ds(pl.multiple_of(at * 64, 64), 64)
-        value = tables32[span, :]
-        high = value.astype(jnp.bfloat16)
-        tables[0, span, :] = high
-        tables[1, span, :] = (value - high.astype(jnp.float32)).astype(jnp.bfloat16)
-
+    tail(0)
     pl.semaphore_wait(barrier, greeted + jnp.where(z < n_tp - 1, 1, 0) + jnp.where(z > 0, 1, 0))
     edge_copy().start()
-    for q in range(chunks):
-        tail_copy(q).start()
+    tail_copy(0).start()
     if square:
         for t in range(WINDOW):
             w_tick(t)
@@ -258,13 +247,22 @@
     get_query.wait()
     before_edge(0)
 
-    get_medium.wait()
-
-    @pl.loop(0, chunks)
-    def _(q):
+    get_tables.wait()
+
+    @pl.loop(0, (length + rows) // 64)
+    def _(at):
+        span = pl.ds(pl.multiple_of(at * 64, 64), 64)
+        value = tables32[span, :]
+        high = value.astype(jnp.bfloat16)
+        tables[0, span, :] = high
+        tables[1, span, :] = (value - high.astype(jnp.float32)).astype(jnp.bfloat16)
+
+    def spectrum(q):
         taps_now = medium[:, columns(q)]
         transfer[:, columns(q)] = dot(fwd_hi[:, 0:reach], taps_now) + dot(fwd_lo[:, 0:reach], taps_now)
 
+    get_medium.wait()
+    spectrum(0)
     for copy in get_rest:
         copy.wait()
     edge_copy().wait_recv()
@@ -295,6 +293,17 @@
         filtered = filtered + skip[:, cols] * product[pl.ds(reach, rows), cols].astype(jnp.float32)
         gated[z, q] = (query[...] * filtered).astype(jnp.bfloat16)
         z_sends(0, q, lambda copy: copy.start())
+
+        @pl.when(q == 0)
+        def _():
+            @pl.loop(1, chunks)
+            def _(other):
+                tail(other)
+                tail_copy(other).start()
+
+            @pl.loop(1, chunks)
+            def _(other):
+                spectrum(other)
 
         @pl.when(q + 1 < chunks)
         def _():

time: 53.2 us -> 57.5 us (1.081)
  Pallas kernels: 50.7 us -> 55.5 us
    pallas_call x1, Pallas kernels: 50.7 us -> 55.5 us  [on_device(): pl.pallas_call(functools.partial(kernel, n_ctx, n_tp, taps), out_shape=ja...]
where the time goes in v4:
time: 57.5 us; the launch traced here: 57.4 us
  Pallas kernels  55.5 us (97%)
  local copies, waits for them, and re-layouts  1.87 us (3%)
    pallas_call x1, Pallas kernels, on_device(): pl.pallas_call(functools.partial(kernel, n_ctx, n_tp, taps), out_shape=ja...  55.5 us
    unnamed x1, local copies, waits for them, and re-layouts  1.87 us

profile of v4, /device:TPU:1, one launch (start us, length us, event | category | flops | bytes accessed | tf_op | source)
XLA Modules:
  0.0 57.4 jit_solution(14076095169974864338)
XLA Ops:
  0.0 55.5 %shard_map.73 = bf16[256,1024]{1,0:T(8,128)(2,1)} custom-call(bf16[256,1024]{1,0:T(8,128)(2,1)} %residual_hbm.1, bf16[3,256,1024]{2,1,0:T(8,128)(2,1)} %bitcast.3, bf16[3,7,1024]{2,1,0:T(8,128)(2,1)} %bitcast.4, bf16[128,1024]{1,0:T(8,128)(2,1)} %medium_hbm.1, f32[1,1024]{1,0:T(1,128)} %bitcast.5, bf16[512,1024]{1,0:T(8,128)(2,1)} %weight.1, ...), custom_call_target="tpu_custom_call" | custom-call | flops 2147483648 | bytes 2621440 | tf_op jit(solution)/shard_map/pallas_call | solution.py:403
  55.5 1.9 %copy.9 = bf16[256,1024]{1,0:T(8,128)(2,1)} copy(bf16[256,1024]{1,0:T(8,128)(2,1)} %shard_map.73) | data formatting | bytes 1048576

commit v5 on v3

--- a/solution.py
+++ b/solution.py
@@ -9,9 +9,9 @@
 from jax.sharding import PartitionSpec as P
 
 WIDE = 256
-STEP = 128
+STEP = 64
 PIECES = 8
-WINDOW = 6
+WINDOW = 8
 EDGE = 16
 MESH = pl.DeviceIdType.MESH
 
@@ -35,7 +35,7 @@
     tables_hbm,
     out,
     residual, proj, short, medium, skip, tables32, tables,
-    whole, gated, total, wide, short32, product, transfer, query, spec, spec_hi, spec_lo, edge,
+    whole, gated, total, wide, short32, product, transfer, query, spec, spec_out, edge,
     local_sem, own_sem, w_send, w_recv, z_send, z_recv, edge_send, edge_recv, tail_send, tail_recv,
 ):
     rows, chans = residual.shape[0], proj.shape[2]
@@ -93,8 +93,7 @@
     get_medium = bring(4, medium_hbm, medium)
     get_tables = bring(5, tables_hbm, tables32)
     get_rest = [bring(6, skip_hbm, skip), bring(7, residual_hbm, residual)]
-    fwd_hi, fwd_lo = tables.at[0, 0:length, :], tables.at[1, 0:length, :]
-    inv_hi, inv_lo = tables.at[0, pl.ds(length, rows), :], tables.at[1, pl.ds(length, rows), :]
+    forward, inverse = tables.at[0:length, :], tables.at[pl.ds(length, rows), :]
 
     def columns(q):
         return pl.ds(pl.multiple_of(q * WIDE, WIDE), WIDE)
@@ -235,10 +234,7 @@
     @pl.loop(0, (length + rows) // 64)
     def _(at):
         span = pl.ds(pl.multiple_of(at * 64, 64), 64)
-        value = tables32[span, :]
-        high = value.astype(jnp.bfloat16)
-        tables[0, span, :] = high
-        tables[1, span, :] = (value - high.astype(jnp.float32)).astype(jnp.bfloat16)
+        tables[span, :] = tables32[span, :].astype(jnp.bfloat16)
 
     pl.semaphore_wait(barrier, greeted + jnp.where(z < n_tp - 1, 1, 0) + jnp.where(z > 0, 1, 0))
     edge_copy().start()
@@ -263,7 +259,7 @@
     @pl.loop(0, chunks)
     def _(q):
         taps_now = medium[:, columns(q)]
-        transfer[:, columns(q)] = dot(fwd_hi[:, 0:reach], taps_now) + dot(fwd_lo[:, 0:reach], taps_now)
+        transfer[:, columns(q)] = dot(forward[:, 0:reach], taps_now)
 
     for copy in get_rest:
         copy.wait()
@@ -283,15 +279,13 @@
             product[0:reach, cols] = jnp.zeros((reach, WIDE), jnp.bfloat16)
 
         window = product[:, cols]
-        spec[...] = dot(fwd_hi[...], window) + dot(fwd_lo[...], window)
+        spec[...] = dot(forward[...], window)
         for top in range(0, half, 64):
             a, b = spec[top : top + 64, :], spec[half + top : half + top + 64, :]
             c, d = transfer[top : top + 64, cols], transfer[half + top : half + top + 64, cols]
             for at, value in ((top, a * c - b * d), (half + top, a * d + b * c)):
-                high = value.astype(jnp.bfloat16)
-                spec_hi[at : at + 64, :] = high
-                spec_lo[at : at + 64, :] = (value - high.astype(jnp.float32)).astype(jnp.bfloat16)
-        filtered = dot(inv_hi[...], spec_hi[...]) + dot(inv_hi[...], spec_lo[...]) + dot(inv_lo[...], spec_hi[...])
+                spec_out[at : at + 64, :] = value.astype(jnp.bfloat16)
+        filtered = dot(inverse[...], spec_out[...])
         filtered = filtered + skip[:, cols] * product[pl.ds(reach, rows), cols].astype(jnp.float32)
         gated[z, q] = (query[...] * filtered).astype(jnp.bfloat16)
         z_sends(0, q, lambda copy: copy.start())
@@ -403,7 +397,7 @@
             pltpu.VMEM(medium_filter.shape, medium_filter.dtype),
             pltpu.VMEM((1, chans), skip.dtype),
             pltpu.VMEM(tables.shape, jnp.float32),
-            pltpu.VMEM((2,) + tables.shape, jnp.bfloat16),
+            pltpu.VMEM(tables.shape, jnp.bfloat16),
             pltpu.VMEM((n_ctx * depth, outs), jnp.bfloat16),
             pltpu.VMEM((n_tp, chunks, rows, WIDE), jnp.bfloat16),
             pltpu.VMEM((rows, outs), jnp.float32),
@@ -413,7 +407,6 @@
             pltpu.VMEM((length, chans), jnp.float32),
             pltpu.VMEM((rows, WIDE), jnp.float32),
             pltpu.VMEM((length, WIDE), jnp.float32),
-            pltpu.VMEM((length, WIDE), jnp.bfloat16),
             pltpu.VMEM((length, WIDE), jnp.bfloat16),
             pltpu.VMEM((3, EDGE, chans), jnp.bfloat16),
             dma((8,)),
@@ -428,15 +421,18 @@
             dma((chunks,)),
         ],
         compiler_params=pltpu.CompilerParams(
-            collective_id=0, has_side_effects=True, vmem_limit_bytes=63 * 2**20
+            collective_id=0, has_side_effects=True, vmem_limit_bytes=44 * 2**20
         ),
         cost_estimate=pl.CostEstimate(
             flops=2 * rows * n_ctx * depth * outs, bytes_accessed=2 * rows * chans * 5, transcendentals=0
         ),
-    )(
-        residual, proj.transpose(1, 0, 2), short_filter.transpose(1, 0, 2), medium_filter,
-        skip.reshape(1, chans), out_weight, tables,
-    )
+    )(*(
+        pltpu.with_memory_space_constraint(array, pltpu.HBM)
+        for array in (
+            residual, proj.transpose(1, 0, 2), short_filter.transpose(1, 0, 2), medium_filter,
+            skip.reshape(1, chans), out_weight, tables,
+        )
+    ))
 
 
 def solution(mesh):

time: 53.2 us -> 51.1 us (0.961)
  local copies, waits for them, and re-layouts: 1.87 us -> 0.8 us
  Pallas kernels: 50.7 us -> 49.7 us
    unnamed x1, local copies, waits for them, and re-layouts: 1.87 us -> 0.8 us
    pallas_call x1, Pallas kernels: 50.7 us -> 49.7 us  [on_device(): pl.pallas_call(functools.partial(kernel, n_ctx, n_tp, taps), out_shape=ja...]
where the time goes in v5:
time: 51.1 us; the launch traced here: 50.5 us
  Pallas kernels  49.7 us (97%)
  local copies, waits for them, and re-layouts  0.8 us (2%)
    pallas_call x1, Pallas kernels, on_device(): pl.pallas_call(functools.partial(kernel, n_ctx, n_tp, taps), out_shape=ja...  49.7 us

profile of v5, /device:TPU:1, one launch (start us, length us, event | category | flops | bytes accessed | tf_op | source)
XLA Modules:
  0.0 50.5 jit_solution(5650177240547424925)
XLA Ops:
  0.0 49.7 %shard_map.73 = bf16[256,1024]{1,0:T(8,128)(2,1)S(1)} custom-call(bf16[256,1024]{1,0:T(8,128)(2,1)} %residual_hbm.1, bf16[3,256,1024]{2,1,0:T(8,128)(2,1)} %bitcast.3, bf16[3,7,1024]{2,1,0:T(8,128)(2,1)} %bitcast.4, bf16[128,1024]{1,0:T(8,128)(2,1)} %medium_hbm.1, f32[1,1024]{1,0:T(1,128)} %bitcast.5, bf16[512,1024]{1,0:T(8,128)(2,1)} %weight.1, ...), custom_call_target="tpu_custom_call" | custom-call | flops 2147483648 | bytes 2621440 | tf_op jit(solution)/shard_map/pallas_call | solution.py:388
  49.7 0.8 %copy.9 = bf16[256,1024]{1,0:T(8,128)(2,1)} copy(bf16[256,1024]{1,0:T(8,128)(2,1)S(1)} %shard_map.73) | data formatting | bytes 1048576

commit v6 on v5

--- a/solution.py
+++ b/solution.py
@@ -11,7 +11,7 @@
 WIDE = 256
 STEP = 64
 PIECES = 8
-WINDOW = 8
+WINDOW = 6
 EDGE = 16
 MESH = pl.DeviceIdType.MESH
 
@@ -110,10 +110,15 @@
             send_sem=tail_send.at[q], recv_sem=tail_recv.at[q],
             device_id={"ctx": after}, device_id_type=MESH)
 
-    def z_copy(way, step, q, origin):
+    cut = reach + EDGE
+    spans = [(cut, rows - cut), (0, cut)]
+
+    def z_copy(way, step, piece, origin):
+        part_of, q = piece
+        there = gated.at[origin, q, pl.ds(*spans[part_of]), :]
         return pltpu.make_async_remote_copy(
-            src_ref=gated.at[origin, q], dst_ref=gated.at[origin, q],
-            send_sem=z_send.at[way, step, q], recv_sem=z_recv.at[way, step, q],
+            src_ref=there, dst_ref=there,
+            send_sem=z_send.at[way, step, part_of, q], recv_sem=z_recv.at[way, step, part_of, q],
             device_id={"tp": z + 1 if way == 0 else z - 1}, device_id_type=MESH)
 
     def z_sends(step, q, act):
@@ -213,7 +218,7 @@
         for start, count in spots:
             if start < first:
                 multiply(start, count, cols)
-            query[pl.ds(start, count), :] = mixed(0, start, count, cols)
+            query[pl.ds(start, count), cols] = mixed(0, start, count, cols)
 
     get_short.wait()
     for stream in range(3):
@@ -263,36 +268,46 @@
 
     for copy in get_rest:
         copy.wait()
-    edge_copy().wait_recv()
-    for stream in range(3):
-        wide[stream, 0:EDGE, :] = jnp.where(me > 0, edge[stream].astype(jnp.float32), 0.0)
-
-    @pl.loop(0, chunks)
-    def _(q):
+    def gate(part_of, q, skipped):
         cols = columns(q)
-        multiply(0, EDGE, cols)
-        query[0:EDGE, :] = mixed(0, 0, EDGE, cols)
-        tail_copy(q).wait_recv()
-
-        @pl.when(me == 0)
-        def _():
-            product[0:reach, cols] = jnp.zeros((reach, WIDE), jnp.bfloat16)
-
-        window = product[:, cols]
-        spec[...] = dot(forward[...], window)
+        start, count = spans[part_of]
+        window = product[skipped:, cols]
+        spec[...] = dot(forward[:, skipped:], window)
         for top in range(0, half, 64):
             a, b = spec[top : top + 64, :], spec[half + top : half + top + 64, :]
             c, d = transfer[top : top + 64, cols], transfer[half + top : half + top + 64, cols]
             for at, value in ((top, a * c - b * d), (half + top, a * d + b * c)):
                 spec_out[at : at + 64, :] = value.astype(jnp.bfloat16)
-        filtered = dot(inverse[...], spec_out[...])
-        filtered = filtered + skip[:, cols] * product[pl.ds(reach, rows), cols].astype(jnp.float32)
-        gated[z, q] = (query[...] * filtered).astype(jnp.bfloat16)
-        z_sends(0, q, lambda copy: copy.start())
+        filtered = dot(inverse[pl.ds(start, count), :], spec_out[...])
+        filtered = filtered + skip[:, cols] * product[pl.ds(reach + start, count), cols].astype(jnp.float32)
+        gated[z, q, pl.ds(start, count), :] = (query[pl.ds(start, count), cols] * filtered).astype(jnp.bfloat16)
+        z_sends(0, (part_of, q), lambda copy: copy.start())
+
+    @pl.loop(0, chunks)
+    def _(q):
+        product[pl.ds(reach, EDGE), columns(q)] = jnp.zeros((EDGE, WIDE), jnp.bfloat16)
+        gate(0, q, reach)
 
         @pl.when(q + 1 < chunks)
         def _():
             before_edge(q + 1)
+
+    edge_copy().wait_recv()
+    for stream in range(3):
+        wide[stream, 0:EDGE, :] = jnp.where(me > 0, edge[stream].astype(jnp.float32), 0.0)
+
+    @pl.loop(0, chunks)
+    def _(q):
+        cols = columns(q)
+        multiply(0, EDGE, cols)
+        query[0:EDGE, cols] = mixed(0, 0, EDGE, cols)
+        tail_copy(q).wait_recv()
+
+        @pl.when(me == 0)
+        def _():
+            product[0:reach, cols] = jnp.zeros((reach, WIDE), jnp.bfloat16)
+
+        gate(1, q, 0)
 
     def project(origin, begin, count):
         @pl.loop(0, outs // WIDE)
@@ -310,14 +325,14 @@
 
     if square:
         far = corner // 2
-        events = [(step, q) for step in range(n_tp - 2) for q in range(chunks)]
+        events = [(step, (part_of, q)) for step in range(n_tp - 2) for part_of in range(2) for q in range(chunks)]
         for t in range(ticks):
+            for event in events[2 * t : 2 * t + 2]:
+                z_pass(*event)
             w_take(t)
             if t + WINDOW < ticks:
                 w_tick(t + WINDOW)
-            if 1 <= t <= len(events):
-                z_pass(*events[t - 1])
-            if t == len(events):
+            if t == PIECES:
                 own.wait()
                 for piece in range(PIECES):
                     w_copy(4 * ticks + piece, core, piece, core).wait_recv()
@@ -340,7 +355,12 @@
         for step in range(n_tp - 2):
             @pl.loop(0, chunks)
             def _(q):
-                z_pass(step, q)
+                z_pass(step, (0, q))
+
+            @pl.loop(0, chunks)
+            def _(q):
+                z_pass(step, (1, q))
+
         own.wait()
 
         @pl.loop(1, n_ctx)
@@ -354,7 +374,9 @@
                 project(origin, 0, chunks)
 
     for q in range(chunks):
-        z_wait(n_tp - 2, q)
+        z_wait(n_tp - 2, (0, q))
+    for q in range(chunks):
+        z_wait(n_tp - 2, (1, q))
 
         @pl.when((z == 0) | (z == n_tp - 1))
         def _():
@@ -375,7 +397,8 @@
     for step in range(n_tp - 1):
         @pl.loop(0, chunks)
         def _(q):
-            z_sends(step, q, lambda copy: copy.wait_send())
+            for part_of in range(2):
+                z_sends(step, (part_of, q), lambda copy: copy.wait_send())
 
 
 def on_device(n_ctx, n_tp, residual, proj, short_filter, medium_filter, skip, out_weight):
@@ -405,7 +428,7 @@
             pltpu.VMEM((3, 8, chans), jnp.float32),
             pltpu.VMEM((length, chans), jnp.bfloat16),
             pltpu.VMEM((length, chans), jnp.float32),
-            pltpu.VMEM((rows, WIDE), jnp.float32),
+            pltpu.VMEM((rows, chans), jnp.float32),
             pltpu.VMEM((length, WIDE), jnp.float32),
             pltpu.VMEM((length, WIDE), jnp.bfloat16),
             pltpu.VMEM((3, EDGE, chans), jnp.bfloat16),
@@ -413,8 +436,8 @@
             dma,
             dma((max(n_ctx, 7 * PIECES),)),
             dma((max(n_ctx, 7 * PIECES),)),
-            dma((2, n_tp - 1, chunks)),
-            dma((2, n_tp - 1, chunks)),
+            dma((2, n_tp - 1, 2, chunks)),
+            dma((2, n_tp - 1, 2, chunks)),
             dma,
             dma,
             dma((chunks,)),

time: 51.1 us -> 51.6 us (level)
  no operation moved by 1% of the time
where the time goes in v6:
time: 51.6 us; the launch traced here: 51 us
  Pallas kernels  50.2 us (97%)
  local copies, waits for them, and re-layouts  0.8 us (2%)
    pallas_call x1, Pallas kernels, on_device(): pl.pallas_call(functools.partial(kernel, n_ctx, n_tp, taps), out_shape=ja...  50.2 us

profile of v6, /device:TPU:1, one launch (start us, length us, event | category | flops | bytes accessed | tf_op | source)
XLA Modules:
  0.0 51.0 jit_solution(13111897225414146010)
XLA Ops:
  0.0 50.2 %shard_map.73 = bf16[256,1024]{1,0:T(8,128)(2,1)S(1)} custom-call(bf16[256,1024]{1,0:T(8,128)(2,1)} %residual_hbm.1, bf16[3,256,1024]{2,1,0:T(8,128)(2,1)} %bitcast.3, bf16[3,7,1024]{2,1,0:T(8,128)(2,1)} %bitcast.4, bf16[128,1024]{1,0:T(8,128)(2,1)} %medium_hbm.1, f32[1,1024]{1,0:T(1,128)} %bitcast.5, bf16[512,1024]{1,0:T(8,128)(2,1)} %weight.1, ...), custom_call_target="tpu_custom_call" | custom-call | flops 2147483648 | bytes 2621440 | tf_op jit(solution)/shard_map/pallas_call | solution.py:411
  50.2 0.8 %copy.9 = bf16[256,1024]{1,0:T(8,128)(2,1)} copy(bf16[256,1024]{1,0:T(8,128)(2,1)S(1)} %shard_map.73) | data formatting | bytes 1048576

commit v7 on v6

--- a/solution.py
+++ b/solution.py
@@ -323,6 +323,11 @@
     def near(origin):
         return (origin - z <= n_tp - 2) & (z - origin <= n_tp - 2)
 
+    def last_z():
+        for part_of in range(2):
+            for q in range(chunks):
+                z_wait(n_tp - 2, (part_of, q))
+
     if square:
         far = corner // 2
         events = [(step, (part_of, q)) for step in range(n_tp - 2) for part_of in range(2) for q in range(chunks)]
@@ -345,12 +350,15 @@
                     def _():
                         project(origin, 0, chunks)
 
+        last_z()
+
+        @pl.when(((z == 0) | (z == n_tp - 1)) & (n_tp - 1 - z != far))
+        def _():
+            project(n_tp - 1 - z, 0, chunks)
+
         for late in range(PIECES, ticks):
             w_core(late)
-
-        @pl.when(near(far))
-        def _():
-            project(far, 0, chunks)
+        project(far, 0, chunks)
     else:
         for step in range(n_tp - 2):
             @pl.loop(0, chunks)
@@ -373,14 +381,11 @@
             def _():
                 project(origin, 0, chunks)
 
-    for q in range(chunks):
-        z_wait(n_tp - 2, (0, q))
-    for q in range(chunks):
-        z_wait(n_tp - 2, (1, q))
+        last_z()
 
         @pl.when((z == 0) | (z == n_tp - 1))
         def _():
-            project(n_tp - 1 - z, q, 1)
+            project(n_tp - 1 - z, 0, chunks)
 
     out[...] = total[...].astype(jnp.bfloat16)
 

time: 51.6 us -> 49.4 us (0.957)
  Pallas kernels: 50.2 us -> 48.3 us
    pallas_call x1, Pallas kernels: 50.2 us -> 48.3 us  [on_device(): pl.pallas_call(functools.partial(kernel, n_ctx, n_tp, taps), out_shape=ja...]
where the time goes in v7:
time: 49.4 us; the launch traced here: 49.1 us
  Pallas kernels  48.3 us (98%)
  local copies, waits for them, and re-layouts  0.8 us (2%)
    pallas_call x1, Pallas kernels, on_device(): pl.pallas_call(functools.partial(kernel, n_ctx, n_tp, taps), out_shape=ja...  48.3 us

profile of v7, /device:TPU:1, one launch (start us, length us, event | category | flops | bytes accessed | tf_op | source)
XLA Modules:
  0.0 49.1 jit_solution(9972834944625896088)
XLA Ops:
  0.0 48.3 %shard_map.73 = bf16[256,1024]{1,0:T(8,128)(2,1)S(1)} custom-call(bf16[256,1024]{1,0:T(8,128)(2,1)} %residual_hbm.1, bf16[3,256,1024]{2,1,0:T(8,128)(2,1)} %bitcast.3, bf16[3,7,1024]{2,1,0:T(8,128)(2,1)} %bitcast.4, bf16[128,1024]{1,0:T(8,128)(2,1)} %medium_hbm.1, f32[1,1024]{1,0:T(1,128)} %bitcast.5, bf16[512,1024]{1,0:T(8,128)(2,1)} %weight.1, ...), custom_call_target="tpu_custom_call" | custom-call | flops 2147483648 | bytes 2621440 | tf_op jit(solution)/shard_map/pallas_call | solution.py:416
  48.3 0.8 %copy.9 = bf16[256,1024]{1,0:T(8,128)(2,1)} copy(bf16[256,1024]{1,0:T(8,128)(2,1)S(1)} %shard_map.73) | data formatting | bytes 1048576
